TPU v7x, 256 devices: a whole 4x4x8 slice. The times are simulated.
256 devices in a mesh: blk: 32 (over x_lo, z, core), tp: 8 (over y, x_hi).
Axes of the slice: x: 4 (x_hi: 2, x_lo: 2; x = x_hi * 2 + x_lo), y: 4, z: 8, core: 2. Of those that a mesh axis runs over, the one named last changes fastest.
Arguments:
- step_index: int32 [1], replicated, may hold values from 0 to 999
- patch_ids: int32 [32, 2, 512], P('blk'), may hold values from 0 to 255
- noisy_pool: bfloat16 [8192, 2048], P('blk'), may hold values from -6 to 6
- clean_pool: bfloat16 [8192, 2048], P('blk'), may hold values from -6 to 6
- norm_gain: bfloat16 [2048], replicated, may hold values from 0.099609375 to 1.8984375
- q_weight: bfloat16 [2048, 2048], P(None, 'tp'), may hold values from -480 to 480
- k_weight: bfloat16 [2048, 2048], P(None, 'tp'), may hold values from -6 to 6
- value_weight: bfloat16 [65536, 2048], P('blk', 'tp'), may hold values from -6 to 6
- out_weight: bfloat16 [65536, 2048], P(('blk', 'tp')), may hold values from -6 to 6
- value_m: bfloat16 [65536, 2048], P('blk', 'tp'), may hold values from -1.5 to 1.5
- value_v: bfloat16 [65536, 2048], P('blk', 'tp'), may hold values from 0.0009994507 to 0.099609375
- out_m: bfloat16 [65536, 2048], P(('blk', 'tp')), may hold values from -1.5 to 1.5
- out_v: bfloat16 [65536, 2048], P(('blk', 'tp')), may hold values from 0.0009994507 to 0.099609375
Outputs:
- new_value_weight: bfloat16 [65536, 2048], P('blk', 'tp')
- new_out_weight: bfloat16 [65536, 2048], P(('blk', 'tp'))
- token_loss: float32 [64, 512], P('blk', 'tp')
Inputs may be any that keep to these rules, and one draw needn't show every extreme that they name: `patch_ids`: row numbers within the replica's own block of pool rows.
All inputs are finite; a program needn't handle non-finite values.
Results may differ from a plain program's by a relative error of at most 0.0086.
The roundings to bfloat16 on the way count: a program that leaves them out, or rounds other values in their place, can miss the bound.
Values may be sent and summed in bfloat16 or wider, within the bound.
A program may use at most 128 MiB of HBM per device.

v0:
```python
import functools

import jax
import jax.numpy as jnp
from jax import lax
from jax.experimental import pallas as pl
from jax.experimental.pallas import tpu as pltpu
from jax.sharding import PartitionSpec as P

HEAD = 128
CHUNKS = 4

beta_one = 0.9
beta_two = 0.95
learn_rate = 0.05
decay_rate = 0.1
epsilon = 1e-08

BF = jnp.bfloat16
F32 = jnp.float32
MESH = pl.DeviceIdType.MESH
NT = (((1,), (1,)), ((), ()))
TN = (((0,), (0,)), ((), ()))


def dot(a, b):
    return jnp.dot(a, b, preferred_element_type=F32)


def dotg(a, b, dims):
    return lax.dot_general(a, b, dims, preferred_element_type=F32)


def window(i, n):
    return pl.ds(pl.multiple_of(i * n, n), n)


def kernel(
    start,
    n_blk,
    groups,
    ids_ref,
    gain_ref,
    noisy,
    clean,
    q,
    k,
    v,
    o,
    vm,
    vv,
    om,
    ov,
    v_out,
    o_out,
    loss_out,
    xb,
    cb,
    qb,
    kb,
    v0,
    o0,
    v1,
    o1,
    v2,
    o2,
    vmb,
    vvb,
    omb,
    ovb,
    pv,
    po,
    nb,
    nt,
    sc,
    pb,
    mx,
    mt,
    cc,
    gm,
    gw,
    gbv,
    gbo,
    lacc,
    sb,
    rb,
    go,
    lb,
    load_sem,
    out_sem,
    ex_send,
    ex_recv,
    rs_send,
    rs_recv,
    ag_send,
    ag_recv,
    ls_send,
    ls_recv,
):
    blk = lax.axis_index("blk")
    rank = lax.axis_index("tp")
    nbits = n_blk.bit_length() - 1
    rows, dim = xb.shape
    inner = qb.shape[1]
    heads = inner // HEAD
    width = dim // CHUNKS
    own = rows // groups
    in_scale = dim ** (-0.5)
    out_scale = (inner * groups) ** (-0.5)
    score_scale = HEAD ** (-0.5)
    to, behind = [], []
    for s in range(2):
        distance = 1 << ((start + s) % nbits)
        to.append((lax.rem(blk + distance, n_blk), rank))
        behind.append((lax.rem(blk + n_blk - distance, n_blk), rank))
    mine = window(rank, own)

    def partner(j):
        return lax.rem(rank + j, groups)

    loads = {}
    for i, (name, src, dst) in enumerate(
        (
            ("x", noisy, xb),
            ("q", q, qb),
            ("k", k, kb),
            ("v", v, v0),
            ("o", o, o0),
            ("c", clean.at[mine], cb),
            ("vm", vm, vmb),
            ("vv", vv, vvb),
            ("om", om, omb),
            ("ov", ov, ovb),
        )
    ):
        loads[name] = pltpu.make_async_copy(src, dst, load_sem.at[i])
        loads[name].start()

    barrier = pltpu.get_barrier_semaphore()
    greeted = [to[0], to[1], behind[0], behind[1]] + [(blk, partner(j)) for j in range(1, groups)]
    for device in greeted:
        pl.semaphore_signal(barrier, inc=1, device_id=device, device_id_type=MESH)
    pl.semaphore_wait(barrier, len(greeted))

    def exchange_v(s):
        return pltpu.make_async_remote_copy(
            src_ref=v if s == 0 else v1,
            dst_ref=pv.at[s],
            send_sem=ex_send.at[s, CHUNKS],
            recv_sem=ex_recv.at[s, CHUNKS],
            device_id=to[s],
            device_id_type=MESH,
        )

    def exchange_o0():
        return pltpu.make_async_remote_copy(
            src_ref=o,
            dst_ref=po.at[0],
            send_sem=ex_send.at[0, 0],
            recv_sem=ex_recv.at[0, 0],
            device_id=to[0],
            device_id_type=MESH,
        )

    def exchange_o1(c):
        cols = window(c, width)
        return pltpu.make_async_remote_copy(
            src_ref=o1.at[:, cols],
            dst_ref=po.at[1, :, cols],
            send_sem=ex_send.at[1, c],
            recv_sem=ex_recv.at[1, c],
            device_id=to[1],
            device_id_type=MESH,
        )

    exchange_v(0).start()
    exchange_o0().start()

    def rs_copy(s, c, j):
        t = partner(j)
        return pltpu.make_async_remote_copy(
            src_ref=sb.at[s, c, window(t, own)],
            dst_ref=rb.at[s, c, j],
            send_sem=rs_send.at[s, c, j],
            recv_sem=rs_recv.at[s, c, j],
            device_id=(blk, t),
            device_id_type=MESH,
        )

    def ag_copy(s, c, j):
        return pltpu.make_async_remote_copy(
            src_ref=go.at[s, c, mine],
            dst_ref=go.at[s, c, mine],
            send_sem=ag_send.at[s, c, j],
            recv_sem=ag_recv.at[s, c, j],
            device_id=(blk, partner(j)),
            device_id_type=MESH,
        )

    def ls_copy(s, j):
        return pltpu.make_async_remote_copy(
            src_ref=lb.at[s, mine],
            dst_ref=lb.at[s, mine],
            send_sem=ls_send.at[s, j],
            recv_sem=ls_recv.at[s, j],
            device_id=(blk, partner(j)),
            device_id_type=MESH,
        )

    def each(n, fn):
        def step(i, carry):
            fn(i)
            return carry

        lax.fori_loop(0, n, step, 0)

    def present(s):
        return lax.broadcasted_iota(jnp.int32, (rows, ids_ref.shape[1]), 0) == ids_ref[s : s + 1, :]

    def weighted(x, s):
        return (x.astype(F32) * cc[s]).astype(BF)

    loads["x"].wait()
    tile = 16

    def norm_tile(i):
        at = window(i, tile)
        wide = xb[at, :].astype(F32)
        mean_sq = jnp.mean(wide * wide, axis=-1, keepdims=True)
        nb[at, :] = (wide * lax.rsqrt(mean_sq + 1e-05) * gain_ref[...].astype(F32)).astype(BF)

    each(rows // tile, norm_tile)
    loads["q"].wait()
    queries = (dot(nb[...], qb[...]) * in_scale).astype(BF)
    loads["k"].wait()
    keys = (dot(nb[...], kb[...]) * in_scale).astype(BF)
    for h in range(heads):
        at = slice(h * HEAD, (h + 1) * HEAD)
        sc[h] = dotg(queries[:, at], keys[:, at], NT) * score_scale

    def probabilities(s):
        hot = present(s).astype(F32)
        column = jnp.sum(hot, axis=1, keepdims=True)
        cc[s] = jnp.broadcast_to(column, (rows, inner))
        line = dotg(jnp.ones((8, hot.shape[1]), BF), hot.astype(BF), NT)[0:1, :]
        for h in range(heads):
            score = jnp.where(line > 0.0, sc[h], -jnp.inf)
            expo = jnp.exp(score - jnp.max(score, axis=-1, keepdims=True))
            total = jnp.sum(expo * line, axis=-1, keepdims=True)
            pb[s, h] = (expo / total).astype(BF)

    def mix(s, weight):
        values = weighted((dot(nb[...], weight[...]) * in_scale).astype(BF), s)
        for h in range(heads):
            at = slice(h * HEAD, (h + 1) * HEAD)
            mx[s, :, at] = dot(pb[s, h], values[:, at]).astype(BF)

    def mix_turned(s):
        mt[s] = (mx[s].astype(F32) * cc[s]).T.astype(BF)

    def partial_chunk(s, weight, c):
        part = dot(mx[s], weight[:, window(c, width)]) * out_scale
        sb[s, c] = part.astype(BF)
        each(groups - 1, lambda j: rs_copy(s, c, j + 1).start())

    def reduce_chunk(s, c):
        cols = window(c, width)
        each(groups - 1, lambda j: rs_copy(s, c, j + 1).wait_recv())
        summed = sb[s, c, mine].astype(F32)
        for j in range(1, groups):
            summed = summed + rb[s, c, j].astype(F32)
        error = xb[mine, cols].astype(F32) + summed - cb[:, cols].astype(F32)
        lacc[...] = lacc[...] + jnp.sum(error * error, axis=-1, keepdims=True)
        go[s, c, mine] = error.astype(BF)
        each(groups - 1, lambda j: ag_copy(s, c, j + 1).start())

    def error_parts(s):
        lacc[...] = jnp.zeros_like(lacc)
        each(CHUNKS, functools.partial(reduce_chunk, s))
        lb[s, mine] = lacc[...] * (1.0 / dim)
        each(groups - 1, lambda j: ls_copy(s, j + 1).start())

    def grad_mixed_chunk(s, weight, c):
        each(groups - 1, lambda j: ag_copy(s, c, j + 1).wait_recv())
        gm[...] = gm[...] + dotg(go[s, c], weight[:, window(c, width)], NT)

    def grad_values(s, weight):
        gm[...] = jnp.zeros_like(gm)
        each(CHUNKS, functools.partial(grad_mixed_chunk, s, weight))
        grad_mixed = weighted((gm[...] * out_scale).astype(BF), s)
        for h in range(heads):
            at = slice(h * HEAD, (h + 1) * HEAD)
            gw[:, at] = weighted_half(dotg(pb[s, h], grad_mixed[:, at], TN).astype(BF), s)

    def weighted_half(x, s):
        return (x.astype(F32) * cc[s, :, :HEAD]).astype(BF)

    def adam(grad, moment, second, old, peer, new, keep, at):
        g = grad
        first = beta_one * moment[at].astype(F32) + (1.0 - beta_one) * g
        square = beta_two * second[at].astype(F32) + (1.0 - beta_two) * g * g
        middle = 0.5 * (old[at].astype(F32) + peer[at].astype(F32))
        updated = middle - learn_rate * (first / (jnp.sqrt(square) + epsilon) + decay_rate * middle)
        new[at] = updated.astype(BF)
        if keep:
            moment[at] = first.astype(BF)
            second[at] = square.astype(BF)

    def update_v_chunk(s, old, new, i):
        step = dim // CHUNKS
        gbv[...] = dot(nt[window(i, step), :], gw[...]) * in_scale

        def one(t):
            adam(gbv[window(t, 32), :], vmb, vvb, old, pv.at[s], new, s == 0, (pl.ds(pl.multiple_of(i * step + t * 32, 32), 32), slice(None)))

        each(step // 32, one)

    def update_o_chunk(s, old, new, c):
        gbo[...] = dot(mt[s], go[s, c]) * out_scale

        def one(t):
            adam(gbo[window(t, tile), :], omb, ovb, old, po.at[s], new, s == 0, (window(t, tile), window(c, width)))

        each(inner // tile, one)

    probabilities(0)
    loads["v"].wait()
    mix(0, v0)
    loads["o"].wait()
    each(CHUNKS, functools.partial(partial_chunk, 0, o0))
    probabilities(1)
    mix_turned(0)

    def turn(i):
        nt[window(i, rows), :] = nb[:, window(i, rows)].astype(F32).T.astype(BF)

    each(dim // rows, turn)
    loads["c"].wait()
    error_parts(0)
    grad_values(0, o0)
    for name in ("vm", "vv", "om", "ov"):
        loads[name].wait()
    exchange_v(0).wait_recv()
    each(CHUNKS, functools.partial(update_v_chunk, 0, v0, v1))
    exchange_v(1).start()

    mix(1, v1)
    exchange_o0().wait_recv()

    def next_chunk(c):
        update_o_chunk(0, o0, o1, c)
        exchange_o1(c).start()
        partial_chunk(1, o1, c)

    each(CHUNKS, next_chunk)
    mix_turned(1)
    error_parts(1)
    grad_values(1, o1)
    exchange_v(1).wait_recv()

    def out_v(i):
        at = window(i, dim // CHUNKS)
        return pltpu.make_async_copy(v2.at[at, :], v_out.at[at, :], out_sem.at[0, i])

    def out_o(c):
        cols = window(c, width)
        return pltpu.make_async_copy(o2.at[:, cols], o_out.at[:, cols], out_sem.at[1, c])

    def last_v(i):
        update_v_chunk(1, v1, v2, i)
        out_v(i).start()

    each(CHUNKS, last_v)

    def last_o(c):
        exchange_o1(c).wait_recv()
        update_o_chunk(1, o1, o2, c)
        out_o(c).start()

    each(CHUNKS, last_o)

    share = loss_out.shape[1]
    for s in range(2):
        each(groups - 1, lambda j: ls_copy(s, j + 1).wait_recv())
        picked = jnp.sum(jnp.where(present(s), lb[s][:, 0:1], 0.0), axis=0, keepdims=True)
        chosen = jnp.zeros((1, share), F32)
        for g in range(groups):
            chosen = jnp.where(rank == g, picked[:, g * share : (g + 1) * share], chosen)
        loss_out[s : s + 1, :] = chosen

    exchange_v(0).wait_send()
    exchange_o0().wait_send()
    exchange_v(1).wait_send()
    each(CHUNKS, lambda c: exchange_o1(c).wait_send())
    for s in range(2):

        def sent(c):
            each(groups - 1, lambda j: rs_copy(s, c, j + 1).wait_send())
            each(groups - 1, lambda j: ag_copy(s, c, j + 1).wait_send())

        each(CHUNKS, sent)
        each(groups - 1, lambda j: ls_copy(s, j + 1).wait_send())
    each(CHUNKS, lambda i: out_v(i).wait())
    each(CHUNKS, lambda c: out_o(c).wait())


def train(start, ids, gain, noisy, clean, q, k, v, o, vm, vv, om, ov):
    n_blk, groups = lax.axis_size("blk"), lax.axis_size("tp")
    rows, dim = noisy.shape
    inner = q.shape[1]
    width = dim // CHUNKS
    own = rows // groups
    vec = pl.BlockSpec(memory_space=pltpu.VMEM)
    hbm = pl.BlockSpec(memory_space=pl.ANY)
    V = pltpu.VMEM
    dma = pltpu.SemaphoreType.DMA
    tall, flat = V((dim, inner), BF), V((inner, dim), BF)
    return pl.pallas_call(
        functools.partial(kernel, start, n_blk, groups),
        out_shape=(
            jax.ShapeDtypeStruct(v.shape, BF),
            jax.ShapeDtypeStruct(o.shape, BF),
            jax.ShapeDtypeStruct((2, ids.shape[1] // groups), F32),
        ),
        in_specs=[vec, vec] + [hbm] * 10,
        out_specs=(hbm, hbm, vec),
        scratch_shapes=[
            V((rows, dim), BF),
            V((own, dim), BF),
            tall,
            tall,
            tall,
            flat,
            tall,
            flat,
            tall,
            flat,
            tall,
            tall,
            flat,
            flat,
            V((2, dim, inner), BF),
            V((2, inner, dim), BF),
            V((rows, dim), BF),
            V((dim, rows), BF),
            V((inner // HEAD, rows, rows), F32),
            V((2, inner // HEAD, rows, rows), BF),
            V((2, rows, inner), BF),
            V((2, inner, rows), BF),
            V((2, rows, inner), F32),
            V((rows, inner), F32),
            V((rows, inner), BF),
            V((dim // CHUNKS, inner), F32),
            V((inner, width), F32),
            V((own, 128), F32),
            V((2, CHUNKS, rows, width), BF),
            V((2, CHUNKS, groups, own, width), BF),
            V((2, CHUNKS, rows, width), BF),
            V((2, rows, 128), F32),
            dma((10,)),
            dma((2, CHUNKS)),
            dma((2, CHUNKS + 1)),
            dma((2, CHUNKS + 1)),
            dma((2, CHUNKS, groups)),
            dma((2, CHUNKS, groups)),
            dma((2, CHUNKS, groups)),
            dma((2, CHUNKS, groups)),
            dma((2, groups)),
            dma((2, groups)),
        ],
        compiler_params=pltpu.CompilerParams(
            collective_id=start, has_side_effects=True, vmem_limit_bytes=56 << 20
        ),
        cost_estimate=pl.CostEstimate(flops=3_200_000_000, bytes_accessed=12 << 20, transcendentals=0),
        name=f"train_{start}",
    )(ids, gain, noisy, clean, q, k, v, o, vm, vv, om, ov)


def on_device(step_index, patch_ids, noisy_pool, clean_pool, norm_gain, q_weight, k_weight, value_weight, out_weight, value_m, value_v, out_m, out_v):
    nbits = lax.axis_size("blk").bit_length() - 1
    return lax.switch(
        step_index[0] % nbits,
        [functools.partial(train, e) for e in range(nbits)],
        patch_ids[0],
        norm_gain[None, :],
        noisy_pool,
        clean_pool,
        q_weight,
        k_weight,
        value_weight,
        out_weight,
        value_m,
        value_v,
        out_m,
        out_v,
    )


def solution(mesh):
    in_specs = (
        P(),
        P("blk", None, None),
        P("blk", None),
        P("blk", None),
        P(),
        P(None, "tp"),
        P(None, "tp"),
        P("blk", "tp"),
        P(("blk", "tp"), None),
        P("blk", "tp"),
        P("blk", "tp"),
        P(("blk", "tp"), None),
        P(("blk", "tp"), None),
    )
    out_specs = (P("blk", "tp"), P(("blk", "tp"), None), P("blk", "tp"))
    return jax.shard_map(on_device, mesh=mesh, in_specs=in_specs, out_specs=out_specs, check_vma=False)
```

profile of v0, /device:TPU:1, one launch (start us, length us, event | category | flops | bytes accessed | tf_op | source)
XLA Modules:
  0.0 176.1 jit_solution(5950877090398968365)
XLA Ops:
  1.3 0.0 copy-start
  1.3 0.7 copy-done
  2.0 0.0 copy-start.1
  2.0 0.7 copy-done.1
  2.7 171.0 %conditional.1 = ((bf16[2048,256]{1,0:T(8,128)(2,1)S(1)}, bf16[256,2048]{1,0:T(8,128)(2,1)S(1)}, f32[2,64]{1,0:T(2,128)S(1)})) conditional(s32[]{:T(128)} %clamp.3, (s32[2,512]{1,0:T(2,128)S(1)}, bf16[1,2048]{1,0:T(2,128)(2,1)S(1)}, bf16[256,2048]{1,0:T(8,128)(2,1)}, bf16[256,2048]{1,0:T(8,128)(2,1)}, ...), branch_computations={%region_0.1_spmd, %region_1.2_spmd, %region_2.3_spmd, %region_3.4_... | conditional | flops 3200000000 | bytes 12582920 | solution.py:481
  2.7 170.7 %train_1.1 = (bf16[2048,256]{1,0:T(8,128)(2,1)S(1)}, bf16[256,2048]{1,0:T(8,128)(2,1)S(1)}, f32[2,64]{1,0:T(2,128)S(1)}) custom-call(s32[2,512]{1,0:T(2,128)S(1)} %get-tuple-element.132.ids_ref, bf16[1,2048]{1,0:T(2,128)(2,1)S(1)} %get-tuple-element.133.gain_ref, bf16[256,2048]{1,0:T(8,128)(2,1)} %get-tuple-element.134.noisy, ...), custom_call_target="tpu_custom_call" | custom-call | flops 3200000000 | bytes 12582912 | tf_op jit(solution)/shard_map/cond/branch_1_fun/train_1/pallas_call | solution.py:418
  173.6 1.0 copy.50
  174.6 1.0 copy.51
  175.6 0.6 copy.52
  (1 shorter events, 0.0 us)
Async XLA Ops:
  1.3 0.7 copy-start
  2.0 0.7 copy-start.1
where the time goes:
time: 176 us
  Pallas kernels  171 us (97%)
  local copies, waits for them, and re-layouts  3.86 us (2%)
    pallas_call x1, Pallas kernels, train(): pl.pallas_call(functools.partial(kernel, start, n_blk, groups), out_shape...  171 us
    unnamed x7, local copies, waits for them, and re-layouts  3.85 us

commit v1 on v0

--- a/solution.py
+++ b/solution.py
@@ -83,19 +83,27 @@
     gbo,
     lacc,
     sb,
-    rb,
+    ry,
+    xs,
+    xr,
+    held,
     go,
     lb,
     load_sem,
     out_sem,
     ex_send,
     ex_recv,
-    rs_send,
-    rs_recv,
-    ag_send,
-    ag_recv,
+    ry_send,
+    ry_recv,
+    rx_send,
+    rx_recv,
+    gx_send,
+    gx_recv,
+    gy_send,
+    gy_recv,
     ls_send,
     ls_recv,
+    grant_sem,
 ):
     blk = lax.axis_index("blk")
     rank = lax.axis_index("tp")
@@ -146,54 +154,78 @@
         return pltpu.make_async_remote_copy(
             src_ref=v if s == 0 else v1,
             dst_ref=pv.at[s],
-            send_sem=ex_send.at[s, CHUNKS],
-            recv_sem=ex_recv.at[s, CHUNKS],
+            send_sem=ex_send.at[s, 0],
+            recv_sem=ex_recv.at[s, 0],
             device_id=to[s],
             device_id_type=MESH,
         )
 
-    def exchange_o0():
-        return pltpu.make_async_remote_copy(
-            src_ref=o,
-            dst_ref=po.at[0],
-            send_sem=ex_send.at[0, 0],
-            recv_sem=ex_recv.at[0, 0],
-            device_id=to[0],
-            device_id_type=MESH,
-        )
-
-    def exchange_o1(c):
-        cols = window(c, width)
-        return pltpu.make_async_remote_copy(
-            src_ref=o1.at[:, cols],
-            dst_ref=po.at[1, :, cols],
-            send_sem=ex_send.at[1, c],
-            recv_sem=ex_recv.at[1, c],
-            device_id=to[1],
-            device_id_type=MESH,
-        )
+    def exchange_o(s):
+        return pltpu.make_async_remote_copy(
+            src_ref=o if s == 0 else o1,
+            dst_ref=po.at[s],
+            send_sem=ex_send.at[s, 1],
+            recv_sem=ex_recv.at[s, 1],
+            device_id=to[s],
+            device_id_type=MESH,
+        )
+
+    far = 1 << start % nbits == n_blk // 4
+    granted = [1 << (start + s) % nbits not in (4, 8) for s in range(2)]
+
+    def send_when_granted(s):
+        pl.semaphore_signal(grant_sem.at[s], inc=1, device_id=behind[s], device_id_type=MESH)
+        pl.semaphore_wait(grant_sem.at[s], 1)
+        exchange_o(s).start()
 
     exchange_v(0).start()
-    exchange_o0().start()
-
-    def rs_copy(s, c, j):
-        t = partner(j)
-        return pltpu.make_async_remote_copy(
-            src_ref=sb.at[s, c, window(t, own)],
-            dst_ref=rb.at[s, c, j],
-            send_sem=rs_send.at[s, c, j],
-            recv_sem=rs_recv.at[s, c, j],
-            device_id=(blk, t),
-            device_id_type=MESH,
-        )
-
-    def ag_copy(s, c, j):
+    if not far and not granted[0]:
+        exchange_o(0).start()
+
+    along = groups // 2
+    y, x = rank // 2, lax.rem(rank, 2)
+    across = (blk, 2 * y + 1 - x)
+    column = window(y, 2 * own)
+
+    def ry_copy(s, c, j):
+        t = lax.rem(y + j, along)
+        return pltpu.make_async_remote_copy(
+            src_ref=sb.at[s, c, window(t, 2 * own)],
+            dst_ref=ry.at[s, c, j],
+            send_sem=ry_send.at[s, c, j],
+            recv_sem=ry_recv.at[s, c, j],
+            device_id=(blk, 2 * t + x),
+            device_id_type=MESH,
+        )
+
+    def rx_copy(s, c):
+        return pltpu.make_async_remote_copy(
+            src_ref=xs.at[s, c],
+            dst_ref=xr.at[s, c],
+            send_sem=rx_send.at[s, c],
+            recv_sem=rx_recv.at[s, c],
+            device_id=across,
+            device_id_type=MESH,
+        )
+
+    def gx_copy(s, c):
         return pltpu.make_async_remote_copy(
             src_ref=go.at[s, c, mine],
             dst_ref=go.at[s, c, mine],
-            send_sem=ag_send.at[s, c, j],
-            recv_sem=ag_recv.at[s, c, j],
-            device_id=(blk, partner(j)),
+            send_sem=gx_send.at[s, c],
+            recv_sem=gx_recv.at[s, c],
+            device_id=across,
+            device_id_type=MESH,
+        )
+
+    def gy_copy(s, c, j):
+        t = lax.rem(y + j, along)
+        return pltpu.make_async_remote_copy(
+            src_ref=go.at[s, c, column],
+            dst_ref=go.at[s, c, column],
+            send_sem=gy_send.at[s, c, j],
+            recv_sem=gy_recv.at[s, c, j],
+            device_id=(blk, 2 * t + x),
             device_id_type=MESH,
         )
 
@@ -207,12 +239,12 @@
             device_id_type=MESH,
         )
 
-    def each(n, fn):
+    def each(n, fn, unroll=1):
         def step(i, carry):
             fn(i)
             return carry
 
-        lax.fori_loop(0, n, step, 0)
+        lax.fori_loop(0, n, step, 0, unroll=unroll)
 
     def present(s):
         return lax.broadcasted_iota(jnp.int32, (rows, ids_ref.shape[1]), 0) == ids_ref[s : s + 1, :]
@@ -261,27 +293,54 @@
     def partial_chunk(s, weight, c):
         part = dot(mx[s], weight[:, window(c, width)]) * out_scale
         sb[s, c] = part.astype(BF)
-        each(groups - 1, lambda j: rs_copy(s, c, j + 1).start())
-
-    def reduce_chunk(s, c):
+        each(along - 1, lambda j: ry_copy(s, c, j + 1).start())
+
+    def sum_along(s, c):
+        each(along - 1, lambda j: ry_copy(s, c, j + 1).wait_recv())
+
+        def total(half):
+            summed = sb[s, c, pl.ds(pl.multiple_of(y * 2 * own + half * own, own), own)].astype(F32)
+            for j in range(1, along):
+                summed = summed + ry[s, c, j, window(half, own)].astype(F32)
+            return summed
+
+        xs[s, c] = total(1 - x).astype(BF)
+        rx_copy(s, c).start()
+        held[c] = total(x)
+
+    def finish_error(s, c):
         cols = window(c, width)
-        each(groups - 1, lambda j: rs_copy(s, c, j + 1).wait_recv())
-        summed = sb[s, c, mine].astype(F32)
-        for j in range(1, groups):
-            summed = summed + rb[s, c, j].astype(F32)
+        rx_copy(s, c).wait_recv()
+        summed = held[c] + xr[s, c].astype(F32)
         error = xb[mine, cols].astype(F32) + summed - cb[:, cols].astype(F32)
+        go[s, c, mine] = error.astype(BF)
+        gx_copy(s, c).start()
         lacc[...] = lacc[...] + jnp.sum(error * error, axis=-1, keepdims=True)
-        go[s, c, mine] = error.astype(BF)
-        each(groups - 1, lambda j: ag_copy(s, c, j + 1).start())
+
+    def pass_on(s, c):
+        gx_copy(s, c).wait_recv()
+        each(along - 1, lambda j: gy_copy(s, c, j + 1).start())
 
     def error_parts(s):
         lacc[...] = jnp.zeros_like(lacc)
-        each(CHUNKS, functools.partial(reduce_chunk, s))
+        sum_along(s, 0)
+        sum_along(s, 1)
+        finish_error(s, 0)
+
+        def middle(i):
+            sum_along(s, i + 2)
+            finish_error(s, i + 1)
+            pass_on(s, i)
+
+        each(CHUNKS - 2, middle)
+        finish_error(s, CHUNKS - 1)
+        pass_on(s, CHUNKS - 2)
+        pass_on(s, CHUNKS - 1)
         lb[s, mine] = lacc[...] * (1.0 / dim)
         each(groups - 1, lambda j: ls_copy(s, j + 1).start())
 
     def grad_mixed_chunk(s, weight, c):
-        each(groups - 1, lambda j: ag_copy(s, c, j + 1).wait_recv())
+        each(along - 1, lambda j: gy_copy(s, c, j + 1).wait_recv())
         gm[...] = gm[...] + dotg(go[s, c], weight[:, window(c, width)], NT)
 
     def grad_values(s, weight):
@@ -313,7 +372,7 @@
         def one(t):
             adam(gbv[window(t, 32), :], vmb, vvb, old, pv.at[s], new, s == 0, (pl.ds(pl.multiple_of(i * step + t * 32, 32), 32), slice(None)))
 
-        each(step // 32, one)
+        each(step // 32, one, 2)
 
     def update_o_chunk(s, old, new, c):
         gbo[...] = dot(mt[s], go[s, c]) * out_scale
@@ -321,7 +380,7 @@
         def one(t):
             adam(gbo[window(t, tile), :], omb, ovb, old, po.at[s], new, s == 0, (window(t, tile), window(c, width)))
 
-        each(inner // tile, one)
+        each(inner // tile, one, 2)
 
     probabilities(0)
     loads["v"].wait()
@@ -337,7 +396,12 @@
     each(dim // rows, turn)
     loads["c"].wait()
     error_parts(0)
+    if granted[0]:
+        send_when_granted(0)
     grad_values(0, o0)
+    if far:
+        exchange_v(0).wait_send()
+        exchange_o(0).start()
     for name in ("vm", "vv", "om", "ov"):
         loads[name].wait()
     exchange_v(0).wait_recv()
@@ -345,16 +409,19 @@
     exchange_v(1).start()
 
     mix(1, v1)
-    exchange_o0().wait_recv()
+    exchange_o(0).wait_recv()
 
     def next_chunk(c):
         update_o_chunk(0, o0, o1, c)
-        exchange_o1(c).start()
         partial_chunk(1, o1, c)
 
     each(CHUNKS, next_chunk)
+    if not granted[1]:
+        exchange_o(1).start()
     mix_turned(1)
     error_parts(1)
+    if granted[1]:
+        send_when_granted(1)
     grad_values(1, o1)
     exchange_v(1).wait_recv()
 
@@ -372,8 +439,9 @@
 
     each(CHUNKS, last_v)
 
+    exchange_o(1).wait_recv()
+
     def last_o(c):
-        exchange_o1(c).wait_recv()
         update_o_chunk(1, o1, o2, c)
         out_o(c).start()
 
@@ -388,15 +456,16 @@
             chosen = jnp.where(rank == g, picked[:, g * share : (g + 1) * share], chosen)
         loss_out[s : s + 1, :] = chosen
 
-    exchange_v(0).wait_send()
-    exchange_o0().wait_send()
-    exchange_v(1).wait_send()
-    each(CHUNKS, lambda c: exchange_o1(c).wait_send())
     for s in range(2):
+        exchange_o(s).wait_send()
+        if s == 1 or not far:
+            exchange_v(s).wait_send()
 
         def sent(c):
-            each(groups - 1, lambda j: rs_copy(s, c, j + 1).wait_send())
-            each(groups - 1, lambda j: ag_copy(s, c, j + 1).wait_send())
+            each(along - 1, lambda j: ry_copy(s, c, j + 1).wait_send())
+            rx_copy(s, c).wait_send()
+            gx_copy(s, c).wait_send()
+            each(along - 1, lambda j: gy_copy(s, c, j + 1).wait_send())
 
         each(CHUNKS, sent)
         each(groups - 1, lambda j: ls_copy(s, j + 1).wait_send())
@@ -454,19 +523,27 @@
             V((inner, width), F32),
             V((own, 128), F32),
             V((2, CHUNKS, rows, width), BF),
-            V((2, CHUNKS, groups, own, width), BF),
+            V((2, CHUNKS, groups // 2, 2 * own, width), BF),
+            V((2, CHUNKS, own, width), BF),
+            V((2, CHUNKS, own, width), BF),
+            V((CHUNKS, own, width), F32),
             V((2, CHUNKS, rows, width), BF),
             V((2, rows, 128), F32),
             dma((10,)),
             dma((2, CHUNKS)),
-            dma((2, CHUNKS + 1)),
-            dma((2, CHUNKS + 1)),
-            dma((2, CHUNKS, groups)),
-            dma((2, CHUNKS, groups)),
-            dma((2, CHUNKS, groups)),
-            dma((2, CHUNKS, groups)),
+            dma((2, 2)),
+            dma((2, 2)),
+            dma((2, CHUNKS, groups // 2)),
+            dma((2, CHUNKS, groups // 2)),
+            dma((2, CHUNKS)),
+            dma((2, CHUNKS)),
+            dma((2, CHUNKS)),
+            dma((2, CHUNKS)),
+            dma((2, CHUNKS, groups // 2)),
+            dma((2, CHUNKS, groups // 2)),
             dma((2, groups)),
             dma((2, groups)),
+            pltpu.SemaphoreType.REGULAR((2,)),
         ],
         compiler_params=pltpu.CompilerParams(
             collective_id=start, has_side_effects=True, vmem_limit_bytes=56 << 20

time: 176 us -> 176 us (level)
  the two profiles are of different devices: /device:TPU:1 before, /device:TPU:64 now
where the time goes in v1:
time: 176 us
  Pallas kernels  170 us (97%)
  local copies, waits for them, and re-layouts  3.86 us (2%)
    pallas_call x1, Pallas kernels, train(): pl.pallas_call(functools.partial(kernel, start, n_blk, groups), out_shape...  170 us
    unnamed x7, local copies, waits for them, and re-layouts  3.85 us

profile of v1, /device:TPU:64, one launch (start us, length us, event | category | flops | bytes accessed | tf_op | source)
XLA Modules:
  0.0 176.2 jit_solution(10925636469897905500)
XLA Ops:
  1.3 0.0 copy-start
  1.3 0.7 copy-done
  2.0 0.0 copy-start.1
  2.0 0.7 copy-done.1
  2.7 171.1 %conditional.1 = ((bf16[2048,256]{1,0:T(8,128)(2,1)S(1)}, bf16[256,2048]{1,0:T(8,128)(2,1)S(1)}, f32[2,64]{1,0:T(2,128)S(1)})) conditional(s32[]{:T(128)} %clamp.3, (s32[2,512]{1,0:T(2,128)S(1)}, bf16[1,2048]{1,0:T(2,128)(2,1)S(1)}, bf16[256,2048]{1,0:T(8,128)(2,1)}, bf16[256,2048]{1,0:T(8,128)(2,1)}, ...), branch_computations={%region_0.1_spmd, %region_1.2_spmd, %region_2.3_spmd, %region_3.4_... | conditional | flops 3200000000 | bytes 12582920 | solution.py:558
  2.7 170.5 %train_1.1 = (bf16[2048,256]{1,0:T(8,128)(2,1)S(1)}, bf16[256,2048]{1,0:T(8,128)(2,1)S(1)}, f32[2,64]{1,0:T(2,128)S(1)}) custom-call(s32[2,512]{1,0:T(2,128)S(1)} %get-tuple-element.132.ids_ref, bf16[1,2048]{1,0:T(2,128)(2,1)S(1)} %get-tuple-element.133.gain_ref, bf16[256,2048]{1,0:T(8,128)(2,1)} %get-tuple-element.134.noisy, ...), custom_call_target="tpu_custom_call" | custom-call | flops 3200000000 | bytes 12582912 | tf_op jit(solution)/shard_map/cond/branch_1_fun/train_1/pallas_call | solution.py:487
  173.7 1.0 copy.50
  174.7 1.0 copy.51
  175.7 0.6 copy.52
  (1 shorter events, 0.0 us)
Async XLA Ops:
  1.3 0.7 copy-start
  2.0 0.7 copy-start.1
